TPU v7x, 32 devices: a whole 2x2x4 slice. The times are simulated.
32 devices in a mesh: group: 2 (over core), expert: 4 (over z), mp: 4 (over y, x).
Axes of the slice: x: 2, y: 2, z: 4, core: 2. Of those that a mesh axis runs over, the one named last changes fastest.
Arguments:
- rows: bfloat16 [2, 256, 2048], P('group', 'expert'), may hold values from -6 to 6
- route: int32 [2, 256, 2], P('group', 'expert'), may hold values from 0 to 3, all different within a row; in each aligned block of 64 rows (0 to 63, 64 to 127, ..., all dimensions but the last counted through in order) at most 64 rows name the same one
- gate_int: int32 [2, 256, 2], P('group', 'expert'), may hold values from 1 to 31
- moe_gain: float32 [2, 2048], P('group'), may hold values from 0.1 to 1.9
- w_in: bfloat16 [2, 4, 2048, 4096], P('group', 'expert', None, 'mp'), may hold values from -0.125 to 0.125
- w_out: bfloat16 [2, 4, 4096, 2048], P('group', 'expert', 'mp'), may hold values from -0.09375 to 0.09375
- attn_gain: float32 [2, 2048], P('group'), may hold values from 0.1 to 1.9
- attn_weight: bfloat16 [2, 2048, 2, 1024], P('group', None, None, 'mp'), may hold values from -0.125 to 0.125
- src_len: int32 [4, 6], P('expert'), may hold values from 1 to 16, 64 in all within a row
- target: int32 [4, 6], P('expert'), may hold values from 0 to 255, as said below
- cache: bfloat16 [256, 16, 2, 1024], P('expert', None, None, 'mp'), may hold values from -128 to 128
- cache_len: int32 [256], P('expert'), may hold values from 1 to 16
Outputs:
- moe_out: bfloat16 [2, 256, 2048], P('group', 'expert')
- step_out: bfloat16 [2, 256, 2048], P('group', 'expert')
Inputs may be any that keep to these rules, and one draw needn't show every extreme that they name: `route`: the rows of one device name one expert at most 64 times. `src_len`: the 6 lengths of one row sum to 64. `target`: all targets are different slots.
All inputs are finite; a program needn't handle non-finite values.
Results may differ from a plain program's by a relative error of at most 0.035.
Values may be sent and summed in bfloat16 or wider, within the bound.
A program may use at most 64 MiB of HBM per device.

v0:
```python
import math

import jax
import jax.numpy as jnp
from jax import lax
from jax.sharding import PartitionSpec as P

HEAD_DIM = 128


def layer_norm(values, gain):
    center = values - jnp.mean(values, axis=-1, keepdims=True)
    spread = jnp.mean(center * center, axis=-1, keepdims=True)
    return center * lax.rsqrt(spread + 1e-05) * gain


def body(
    rows,
    route,
    gate_int,
    moe_gain,
    w_in,
    w_out,
    attn_gain,
    attn_weight,
    src_len,
    target,
    cache,
    cache_len,
):
    experts_count = lax.axis_size("expert")
    row_count = rows.shape[1]
    width = rows.shape[2]
    group_place = lax.axis_index("group")
    expert_place = lax.axis_index("expert")
    capacity = max(2, 4 * row_count // experts_count)
    base = rows[0].astype(jnp.float32)
    normed = layer_norm(base, moe_gain[0]).astype(jnp.bfloat16)
    weights = gate_int[0].astype(jnp.float32)
    weights = weights / jnp.sum(weights, axis=1, keepdims=True)
    flat_dest = route[0].reshape(-1)
    onehot = (flat_dest[:, None] == jnp.arange(experts_count)[None, :]).astype(jnp.int32)
    position = jnp.sum((jnp.cumsum(onehot, axis=0) - 1) * onehot, axis=1)
    flat_index = flat_dest * capacity + position
    pair_index = flat_index.reshape(row_count, 2)
    slot_iota = jnp.arange(experts_count * capacity, dtype=jnp.int32)
    slot_table = (
        (slot_iota[:, None] == pair_index[None, :, 0])
        | (slot_iota[:, None] == pair_index[None, :, 1])
    ).astype(jnp.bfloat16)
    buffer = jnp.dot(slot_table, normed, preferred_element_type=jnp.float32).astype(jnp.bfloat16)
    buffer = buffer.reshape(experts_count, capacity, normed.shape[1])
    hidden = jax.nn.relu(
        jnp.einsum(
            "sci,if->scf",
            lax.all_to_all(buffer, "expert", split_axis=0, concat_axis=0, tiled=True),
            w_in[0, 0],
            preferred_element_type=jnp.float32,
        )
    ).astype(jnp.bfloat16)
    partial_rows = jnp.einsum(
        "scf,fo->sco", hidden, w_out[0, 0], preferred_element_type=jnp.float32
    )
    summed = lax.psum(partial_rows.astype(jnp.bfloat16), "mp")
    returned = lax.all_to_all(summed, "expert", split_axis=0, concat_axis=0, tiled=True)
    returned = returned.reshape(experts_count * capacity, returned.shape[2])
    picked = returned[flat_index].reshape(row_count, 2, returned.shape[1]).astype(jnp.float32)
    added = weights[:, 0:1] * picked[:, 0] + weights[:, 1:2] * picked[:, 1]
    moe_rows = (base + added).astype(jnp.bfloat16)
    encoded = layer_norm(moe_rows.astype(jnp.float32), attn_gain[0]).astype(jnp.bfloat16)
    head_width = attn_weight.shape[3]
    projected = jnp.dot(
        encoded, attn_weight[0].reshape(width, 2 * head_width), preferred_element_type=jnp.float32
    )
    projected = projected.reshape(row_count, 2, head_width).astype(jnp.bfloat16)
    query = projected[:, 0, :]
    lengths = src_len[0]
    ends = jnp.cumsum(lengths)
    starts = ends - lengths
    row_iota = jnp.arange(row_count, dtype=jnp.int32)
    which = jnp.sum((row_iota[:, None] >= ends[None, :]).astype(jnp.int32), axis=1)
    select = which[:, None] == jnp.arange(lengths.shape[0])[None, :]
    row_start = jnp.sum(jnp.where(select, starts[None, :], 0), axis=1)
    row_len = jnp.sum(jnp.where(select, lengths[None, :], 0), axis=1)
    row_slot = jnp.sum(jnp.where(select, target[0][None, :], 0), axis=1)
    row_pos = row_iota - row_start
    positions = cache.shape[1]
    cell_iota = jnp.arange(row_count * positions, dtype=jnp.int32)
    slot_ids = jnp.arange(row_count, dtype=jnp.int32)
    sent_slot = jnp.where(group_place == 0, row_slot, -1)
    slot_kv = cache
    slot_len = cache_len
    kv_piece = lax.all_gather(projected, ("group", "expert"), axis=0, tiled=True)
    slot_piece = lax.all_gather(sent_slot, ("group", "expert"), axis=0, tiled=True)
    pos_piece = lax.all_gather(row_pos, ("group", "expert"), axis=0, tiled=True)
    len_piece = lax.all_gather(row_len, ("group", "expert"), axis=0, tiled=True)
    local = slot_piece - expert_place * row_count
    inside = (local >= 0) & (local < row_count)
    cell = jnp.where(inside, local * positions + pos_piece, -1)
    hit = cell_iota[:, None] == cell[None, :]
    written = jnp.dot(
        hit.astype(jnp.bfloat16),
        kv_piece.reshape(kv_piece.shape[0], -1),
        preferred_element_type=jnp.float32,
    )
    written = written.astype(jnp.bfloat16).reshape(slot_kv.shape)
    touched = jnp.any(hit, axis=1).reshape(row_count, positions)
    slot_kv = jnp.where(touched[:, :, None, None], written, slot_kv)
    slot_hit = (slot_ids[:, None] == local[None, :]) & inside[None, :]
    fresh = jnp.max(jnp.where(slot_hit, len_piece[None, :], 0), axis=1).astype(jnp.int32)
    slot_len = jnp.where(jnp.any(slot_hit, axis=1), fresh, slot_len)
    slot_kv, slot_len = (slot_kv, slot_len)
    heads_here = head_width // HEAD_DIM
    keys = slot_kv[:, :, 0, :].reshape(row_count, positions, heads_here, HEAD_DIM)
    values = slot_kv[:, :, 1, :].reshape(row_count, positions, heads_here, HEAD_DIM)
    heads_query = query.reshape(row_count, heads_here, HEAD_DIM)
    scores = jnp.einsum("thd,tphd->thp", heads_query, keys, preferred_element_type=jnp.float32) * (
        1.0 / math.sqrt(HEAD_DIM)
    )
    inside = jnp.arange(positions)[None, None, :] < slot_len[:, None, None]
    scores = jnp.where(inside, scores, -1e30)
    highest = jnp.max(scores, axis=-1, keepdims=True)
    raised = jnp.where(inside, jnp.exp(scores - highest), 0.0)
    probs = (raised / jnp.sum(raised, axis=-1, keepdims=True)).astype(jnp.bfloat16)
    context = jnp.einsum("thp,tphd->thd", probs, values, preferred_element_type=jnp.float32).astype(
        jnp.bfloat16
    )
    context = context.reshape(row_count, head_width)
    output_map = attn_weight[0][:, 1, :]
    mixed = lax.dot_general(
        context, output_map, (((1,), (1,)), ((), ())), preferred_element_type=jnp.float32
    )
    mixed = lax.psum(mixed.astype(jnp.bfloat16), "mp").astype(jnp.float32)
    decoded = (moe_rows.astype(jnp.float32) + mixed).astype(jnp.bfloat16)
    step_rows = jnp.where(group_place == 0, encoded, decoded)
    return (moe_rows[None], step_rows[None])


def solution(mesh):
    return jax.shard_map(
        body,
        mesh=mesh,
        in_specs=(
            P("group", "expert", None),
            P("group", "expert", None),
            P("group", "expert", None),
            P("group", None),
            P("group", "expert", None, "mp"),
            P("group", "expert", "mp", None),
            P("group", None),
            P("group", None, None, "mp"),
            P("expert", None),
            P("expert", None),
            P("expert", None, None, "mp"),
            P("expert"),
        ),
        out_specs=(P("group", "expert", None), P("group", "expert", None)),
        check_vma=False,
    )
```

profile of v0, /device:TPU:1, one launch (start us, length us, event | category | flops | bytes accessed | tf_op | source)
XLA Modules:
  0.0 229.1 jit_solution(5595939843658151987)
XLA Ops:
  9.5 1.1 convert_reduce_fusion.1
  10.6 1.2 fusion.36
  11.8 2.5 %convolution_convert_fusion = bf16[256,2048]{1,0:T(8,128)(2,1)} fusion(bf16[1,64,2048]{2,1,0:T(8,128)(2,1)} %param.12, f32[2048]{0:T(1024)} %bitcast.160, f32[64]{0:T(128)S(1)} %add_rsqrt_fusion.1, f32[64]{0:T(128)S(1)} %broadcast_multiply_fusion.2, s32[64]{0:T(128)S(1)} %get-tuple-element.19, s32[64]{0:T(128)S(1)} %get-tuple-element.18), kind=kOutput, calls=%fused_computation.8 | convolution fusion | flops 68337664 | bytes 1319936 | tf_op jit(solution)/shard_map/dot_general | solution.py:51
  14.2 5.4 %all-to-all-start = ((bf16[4,64,2048]{2,1,0:T(8,128)(2,1)}), bf16[4,64,2048]{2,1,0:T(8,128)(2,1)S(1)}, u32[]{:S(2)}, u32[]{:S(2)}) async-start(bf16[4,64,2048]{2,1,0:T(8,128)(2,1)} %bitcast.7), calls=%async_computation | async-start | bytes 2097152 | tf_op jit(solution)/shard_map/all_to_all | solution.py:56
  19.8 25.0 %all-to-all-done = bf16[4,64,2048]{2,1,0:T(8,128)(2,1)S(1)} async-done(((bf16[4,64,2048]{2,1,0:T(8,128)(2,1)}), bf16[4,64,2048]{2,1,0:T(8,128)(2,1)S(1)}, u32[]{:S(2)}, u32[]{:S(2)}) %all-to-all-start) | async-done | bytes 1048608 | tf_op jit(solution)/shard_map/all_to_all | solution.py:56
  44.9 6.8 %fusion.6 = bf16[4,64,2048]{2,1,0:T(8,128)(2,1)} fusion(bf16[1,1,1024,2048]{3,2,1,0:T(8,128)(2,1)} %param.17, bf16[4,64,2048]{2,1,0:T(8,128)(2,1)S(1)} %all-to-all-done, bf16[1,1,2048,1024]{3,2,1,0:T(8,128)(2,1)} %param.16), kind=kOutput, calls=%fused_computation.7 | convolution fusion | flops 2148532224 | bytes 10485760 | tf_op jit(solution)/shard_map/scf,fo->sco/dot_general | solution.py:61
  53.6 8.1 %all-reduce.3 = (s32[512]{0:T(512)S(1)}, s32[512]{0:T(512)S(1)}, s32[512]{0:T(512)S(1)}) all-reduce(s32[512]{0:T(512)S(1)} %subtract_dynamic-update-slice_fusion, s32[512]{0:T(512)S(1)} %fusion.77, s32[512]{0:T(512)S(1)} %dynamic-update-slice.1), channel_id=1, replica_groups=mesh['group'=2,'expert'=4,'mp'=4] {'group','expert'}, use_global_device_ids=true, to_apply=%add.2 | all-reduce | flops 1536 | bytes 12288
  61.7 42.6 %all-reduce.7.cloned.1.call-done = bf16[4,64,2048]{2,1,0:T(8,128)(2,1)} async-done(((bf16[4,64,2048]{2,1,0:T(8,128)(2,1)}), bf16[4,64,2048]{2,1,0:T(8,128)(2,1)}) %all-reduce.7.cloned.1.call-update) | async-done | bytes 1048592 | tf_op jit(solution)/shard_map/psum | solution.py:64
  104.3 4.3 %all-to-all-start.1 = ((bf16[4,64,2048]{2,1,0:T(8,128)(2,1)}), bf16[4,64,2048]{2,1,0:T(8,128)(2,1)S(1)}, u32[]{:S(2)}, u32[]{:S(2)}) async-start(bf16[4,64,2048]{2,1,0:T(8,128)(2,1)} %all-reduce.7.cloned.1.call-done), calls=%async_computation.1 | async-start | bytes 2097152 | tf_op jit(solution)/shard_map/all_to_all | solution.py:65
  108.9 1.6 copy.65
  110.5 1.7 copy.44
  112.2 3.0 %copy.31 = bf16[512,2048]{1,0:T(8,128)(2,1)S(1)} copy(bf16[512,2048]{0,1:T(8,128)(2,1)} %bitcast.153) | data formatting | bytes 4194304 | tf_op jit(solution)/shard_map/dot_general | solution.py:72
  116.0 17.9 %all-to-all-done.1 = bf16[4,64,2048]{2,1,0:T(8,128)(2,1)S(1)} async-done(((bf16[4,64,2048]{2,1,0:T(8,128)(2,1)}), bf16[4,64,2048]{2,1,0:T(8,128)(2,1)S(1)}, u32[]{:S(2)}, u32[]{:S(2)}) %all-to-all-start.1) | async-done | bytes 1048608 | tf_op jit(solution)/shard_map/all_to_all | solution.py:65
  133.8 1.7 gather_fusion
  135.6 1.7 reshape.249
  140.1 25.2 %all_gather.15 = bf16[512,2,256]{2,0,1:T(8,128)(2,1)S(1)} all-gather(bf16[64,2,256]{2,0,1:T(8,128)(2,1)S(1)} %convolution_convert_fusion.2), channel_id=1, replica_groups=mesh['group'=2,'expert'=4,'mp'=4] {'group','expert'}, dimensions={0}, use_global_device_ids=true | all-gather | bytes 589824 | tf_op jit(solution)/shard_map/all_gather | solution.py:93
  165.5 1.7 fusion.11
  167.2 1.3 reshape.247
  168.6 1.8 broadcast_select_fusion
  170.4 5.1 %slice_reduce_fusion = (bf16[64,16,256]{2,1,0:T(8,128)(2,1)S(1)}, bf16[64,16,256]{2,1,0:T(8,128)(2,1)}) fusion(bf16[64,16,2,256]{3,2,1,0:T(2,128)(2,1)S(1)} %broadcast_select_fusion), kind=kLoop, calls=%fused_computation.26 | loop fusion | bytes 2097152 | tf_op jit(solution)/shard_map/slice | solution.py:115
  175.5 1.4 fusion.45
  177.5 1.1 convolution_convert_fusion.1
  178.7 41.7 %all-reduce.9.cloned.1.call-done = bf16[64,2048]{1,0:T(8,128)(2,1)} async-done(((bf16[64,2048]{1,0:T(8,128)(2,1)}), bf16[64,2048]{1,0:T(8,128)(2,1)}) %all-reduce.9.cloned.1.call-update) | async-done | bytes 262160 | tf_op jit(solution)/shard_map/psum | solution.py:133
  220.4 1.9 fusion.54
  (84 shorter events, 8.1 us)
Async XLA Ops:
  8.2 11.5 %copy-start.9 = (s32[1,6]{1,0:T(1,128)S(1)}, s32[1,6]{1,0:T(1,128)}, u32[]{:S(2)}) copy-start(s32[1,6]{1,0:T(1,128)} %param.20) | copy-start | bytes 76
  14.2 30.7 %all-to-all-start = ((bf16[4,64,2048]{2,1,0:T(8,128)(2,1)}), bf16[4,64,2048]{2,1,0:T(8,128)(2,1)S(1)}, u32[]{:S(2)}, u32[]{:S(2)}) async-start(bf16[4,64,2048]{2,1,0:T(8,128)(2,1)} %bitcast.7), calls=%async_computation | async-start | bytes 2097152 | tf_op jit(solution)/shard_map/all_to_all | solution.py:56
  19.6 84.7 %all-reduce.7.cloned.1.call-start = ((), (), s32[]{:S(2)}) async-start(), calls=%async_computation.2 | async-start | bytes 2097152 | tf_op jit(solution)/shard_map/psum | solution.py:64
  19.8 31.9 %copy-start.12 = (u32[32]{0:T(128)S(1)}, u32[32]{0:T(128)}, u32[]{:S(2)}) copy-start(u32[32]{0:T(128)} %constant.68) | copy-start | bytes 388
  19.8 33.2 %copy-start.10 = (s32[1,6]{1,0:T(1,128)S(1)}, s32[1,6]{1,0:T(1,128)}, u32[]{:S(2)}) copy-start(s32[1,6]{1,0:T(1,128)} %param.21) | copy-start | bytes 76
  51.7 57.0 %copy-start.7 = (s32[1,64,2]{1,2,0:T(2,128)S(1)}, s32[1,64,2]{1,2,0:T(2,128)}, u32[]{:S(2)}) copy-start(s32[1,64,2]{1,2,0:T(2,128)} %param.13) | copy-start | bytes 1540
  51.7 57.2 %copy-start = (bf16[1,2048,2,256]{3,2,1,0:T(2,128)(2,1)S(1)}, bf16[1,2048,2,256]{3,2,1,0:T(2,128)(2,1)}, u32[]{:S(2)}) copy-start(bf16[1,2048,2,256]{3,2,1,0:T(2,128)(2,1)} %param.19) | copy-start | bytes 6291460
  104.3 29.6 %all-to-all-start.1 = ((bf16[4,64,2048]{2,1,0:T(8,128)(2,1)}), bf16[4,64,2048]{2,1,0:T(8,128)(2,1)S(1)}, u32[]{:S(2)}, u32[]{:S(2)}) async-start(bf16[4,64,2048]{2,1,0:T(8,128)(2,1)} %all-reduce.7.cloned.1.call-done), calls=%async_computation.1 | async-start | bytes 2097152 | tf_op jit(solution)/shard_map/all_to_all | solution.py:65
  108.6 111.8 %all-reduce.9.cloned.1.call-start = ((), (), s32[]{:S(2)}) async-start(), calls=%async_computation.3 | async-start | bytes 524288 | tf_op jit(solution)/shard_map/psum | solution.py:133
  112.2 3.6 %copy-start.11 = (s32[64]{0:T(128)S(1)}, s32[64]{0:T(128)}, u32[]{:S(2)}) copy-start(s32[64]{0:T(128)} %param.23) | copy-start | bytes 772
  112.2 3.6 %copy-start.8 = (s32[1,64,2]{1,2,0:T(2,128)S(1)}, s32[1,64,2]{1,2,0:T(2,128)}, u32[]{:S(2)}) copy-start(s32[1,64,2]{1,2,0:T(2,128)} %param.14) | copy-start | bytes 1540
  135.6 2.6 %copy-start.1 = (bf16[1,64,2048]{2,1,0:T(8,128)(2,1)S(1)}, bf16[1,64,2048]{2,1,0:T(8,128)(2,1)}, u32[]{:S(2)}) copy-start(bf16[1,64,2048]{2,1,0:T(8,128)(2,1)} %param.12) | copy-start | bytes 786436
  138.1 1.2 copy-start.6
  139.0 26.5 %copy-start.4 = (bf16[1,64,2048]{2,1,0:T(8,128)(2,1)}, bf16[1,64,2048]{2,1,0:T(8,128)(2,1)S(1)}, u32[]{:S(2)}) copy-start(bf16[1,64,2048]{2,1,0:T(8,128)(2,1)S(1)} %fusion.40) | copy-start | bytes 786436
  140.1 27.2 %copy-start.5 = (bf16[64,2,256]{2,0,1:T(8,128)(2,1)}, bf16[64,2,256]{2,0,1:T(8,128)(2,1)S(1)}, u32[]{:S(2)}) copy-start(bf16[64,2,256]{2,0,1:T(8,128)(2,1)S(1)} %convolution_convert_fusion.2) | copy-start | bytes 196612
  165.5 3.1 %copy-start.3 = (bf16[64,16,2,256]{3,2,1,0:T(2,128)(2,1)S(1)}, bf16[64,16,2,256]{3,2,1,0:T(2,128)(2,1)}, u32[]{:S(2)}) copy-start(bf16[64,16,2,256]{3,2,1,0:T(2,128)(2,1)} %param.22) | copy-start | bytes 3145732
  170.4 5.1 %slice-start = ((bf16[64,2,256]{2,0,1:T(8,128)(2,1)}), bf16[64,1,256]{2,0,1:T(8,128)(2,1)S(1)}, s32[]{:S(2)}) async-start(bf16[64,2,256]{2,0,1:T(8,128)(2,1)} %copy-done.5), calls=%async_computation.4 | async-start | bytes 65536 | tf_op jit(solution)/shard_map/slice | solution.py:76
  170.4 7.1 %copy-start.2 = (bf16[1,2048,2,256]{3,1,2,0:T(8,128)(2,1)S(1)}, bf16[1,2048,2,256]{3,1,2,0:T(8,128)(2,1)}, u32[]{:S(2)}) copy-start(bf16[1,2048,2,256]{3,1,2,0:T(8,128)(2,1)} %copy.65) | copy-start | bytes 6291460
Sparse Core Ops, SparseCore 0:
  51.8 52.4 all-reduce.6
  178.8 41.4 all-reduce.8
where the time goes:
time: 231 us; the launch traced here: 229 us
  waiting for transfers between devices  127 us (55%)
  blocking collectives  33.3 us (14%)
  local copies, waits for them, and re-layouts  19.8 us (9%)
  between operations  15 us (6%)
  matrix products  14.6 us (6%)
  starting transfers between devices  9.74 us (4%)
  other arithmetic  9.4 us (4%)
    psum x1, waiting for transfers between devices, body(): summed = lax.psum(partial_rows.astype(jnp.bfloat16), 'mp')  42.6 us
    psum x1, waiting for transfers between devices, body(): mixed = lax.psum(mixed.astype(jnp.bfloat16), 'mp').astype(jnp.float32)  41.7 us
    all_gather x1, blocking collectives, body(): lax.all_gather(projected, ('group', 'expert'), axis=0, tiled=True)  25.2 us
    all_to_all x1, waiting for transfers between devices, body(): lax.all_to_all(buffer, 'expert', split_axis=0, concat_axis=0, tiled=True)  25 us
    all_to_all x1, waiting for transfers between devices, body(): lax.all_to_all(summed, 'expert', split_axis=0, concat_axis=0, tiled=True)  17.9 us
    unnamed x1, blocking collectives  8.11 us
    dot_general x1, matrix products, body(): jnp.einsum('scf,fo->sco', hidden, w_out[0, 0], preferred_element_type=jnp...  6.79 us
    all_to_all x1, starting transfers between devices, body(): lax.all_to_all(buffer, 'expert', split_axis=0, concat_axis=0, tiled=True)  5.42 us
  transfers between devices with their start and end apart: 4, of which 4 were waited for; matrix products, arithmetic and copies ran while one was open for 4% of the time, Pallas kernels for 0%

commit v1 on v0

--- a/solution.py
+++ b/solution.py
@@ -3,6 +3,8 @@
 import jax
 import jax.numpy as jnp
 from jax import lax
+from jax.experimental import pallas as pl
+from jax.experimental.pallas import tpu as pltpu
 from jax.sharding import PartitionSpec as P
 
 HEAD_DIM = 128
@@ -14,7 +16,7 @@
     return center * lax.rsqrt(spread + 1e-05) * gain
 
 
-def body(
+def spread_body(
     rows,
     route,
     gate_int,
@@ -136,9 +138,332 @@
     return (moe_rows[None], step_rows[None])
 
 
+MESH = pl.DeviceIdType.MESH
+NT = (((1,), (1,)), ((), ()))
+
+
+def norm_rows(values, gain):
+    center = values - jnp.mean(values, axis=-1, keepdims=True)
+    spread = jnp.mean(center * center, axis=-1, keepdims=True)
+    return (center * lax.rsqrt(spread + 1e-05) * gain).astype(jnp.bfloat16)
+
+
+def kernel(
+    rows_ref, route_ref, gate_ref, moe_gain_ref, attn_gain_ref, src_ref, target_ref, cache_len_ref,
+    w_in_hbm, w_out_hbm, attn_hbm, cache_hbm,
+    moe_ref, step_ref,
+    w_in, w_out, attn, cache, gathered, hidden, part, part_got, summed, back_got, moe, meta,
+    kv, kv_got, slot_kv, mixed, mixed_got, final,
+    load_sem, z_send, z_recv, m_send, m_recv, f_send, f_recv, p_send, p_recv, b_send, b_recv,
+    e_send, e_recv, k_send, k_recv, g_send, g_recv, h_send, h_recv,
+):
+    g = lax.axis_index("group")
+    e = lax.axis_index("expert")
+    m = lax.axis_index("mp")
+    n_expert = lax.axis_size("expert")
+    row_count = rows_ref.shape[1]
+    width = rows_ref.shape[2]
+    quarter = width // 4
+    head_width = attn.shape[1] // 2
+    total = n_expert * row_count
+    y, x = m // 2, m % 2
+    mp_peer = (m, y * 2 + 1 - x, (1 - y) * 2 + x, 3 - m)
+    ahead = [(e + d) % n_expert for d in range(n_expert)]
+    behind = [(e + n_expert - d) % n_expert for d in range(n_expert)]
+
+    loads = [
+        pltpu.make_async_copy(w_in_hbm.at[0, 0], w_in, load_sem.at[0]),
+        pltpu.make_async_copy(w_out_hbm.at[0, 0], w_out, load_sem.at[1]),
+        pltpu.make_async_copy(attn_hbm, attn, load_sem.at[2]),
+        pltpu.make_async_copy(cache_hbm, cache, load_sem.at[3]),
+    ]
+    barrier = pltpu.get_barrier_semaphore()
+    friends = [(g, ahead[d], m) for d in range(1, n_expert)]
+    friends += [(g, e, mp_peer[j]) for j in (1, 2, 3)]
+    friends += [(1 - g, ahead[d], m) for d in range(n_expert)]
+    for friend in friends:
+        pl.semaphore_signal(barrier, inc=1, device_id=friend, device_id_type=MESH)
+    for load in loads:
+        load.start()
+
+    def cols(place):
+        return pl.ds(pl.multiple_of(place * quarter, quarter), quarter)
+
+    def block(d):
+        return pl.ds(d * row_count, row_count)
+
+    def send(src, dst, send_sem, recv_sem, device):
+        copy = pltpu.make_async_remote_copy(
+            src_ref=src, dst_ref=dst, send_sem=send_sem, recv_sem=recv_sem,
+            device_id=device, device_id_type=MESH,
+        )
+        return copy
+
+    pending = []
+
+    def go(*args):
+        copy = send(*args)
+        copy.start()
+        pending.append(copy)
+
+    base = rows_ref[0].astype(jnp.float32)
+    gathered[block(0), :] = norm_rows(base, moe_gain_ref[...])
+    meta[0] = jnp.zeros(meta.shape[1:], jnp.int32)
+    meta[0, 0:1, 0:src_ref.shape[1]] = src_ref[...]
+    meta[0, 1:2, 0:src_ref.shape[1]] = target_ref[...]
+    pl.semaphore_wait(barrier, len(friends))
+
+    for d in (2, 1, 3):
+        go(gathered.at[block(0), cols(m)], gathered.at[block(d), cols(m)],
+           z_send.at[d], z_recv.at[d], (g, ahead[d], m))
+    for d in (1, 2, 3):
+        go(meta.at[0], meta.at[d], m_send.at[d], m_recv.at[d], (g, ahead[d], m))
+    for d in (1, 3, 2):
+        mine = gathered.at[block(d), cols(m)]
+        send(mine, mine, z_send.at[d], z_recv.at[d], (g, ahead[d], m)).wait_recv()
+        for j in (3, 1, 2):
+            go(mine, mine, f_send.at[d, j], f_recv.at[d, j], (g, e, mp_peer[j]))
+    for d in (1, 2, 3):
+        send(meta.at[d], meta.at[d], m_send.at[d], m_recv.at[d], (g, ahead[d], m)).wait_recv()
+    for d in (1, 3, 2):
+        for j in (1, 2, 3):
+            theirs = gathered.at[block(d), cols(mp_peer[j])]
+            send(theirs, theirs, f_send.at[d, j], f_recv.at[d, j], (g, e, mp_peer[j])).wait_recv()
+
+    loads[0].wait()
+    tile = 256
+
+    def first(n, carry):
+        at = pl.ds(pl.multiple_of(n * tile, tile), tile)
+        raw = jnp.dot(gathered[...], w_in[:, at], preferred_element_type=jnp.float32)
+        hidden[:, at] = jnp.maximum(raw, 0.0).astype(jnp.bfloat16)
+        return carry
+
+    lax.fori_loop(0, w_in.shape[1] // tile, first, 0)
+
+    loads[1].wait()
+    for j in (3, 1, 2, 0):
+        part[j] = jnp.dot(
+            hidden[...], w_out[:, cols(mp_peer[j])], preferred_element_type=jnp.float32
+        ).astype(jnp.bfloat16)
+        if j > 0:
+            go(part.at[j], part_got.at[j], p_send.at[j], p_recv.at[j], (g, e, mp_peer[j]))
+    for j in (1, 2, 3):
+        send(part.at[j], part_got.at[j], p_send.at[j], p_recv.at[j], (g, e, mp_peer[j])).wait_recv()
+    for d in (2, 1, 3, 0):
+        at = block(d)
+        whole = part[0, at, :].astype(jnp.float32)
+        for j in (1, 2, 3):
+            whole = whole + part_got[j, at, :].astype(jnp.float32)
+        summed[at, :] = whole.astype(jnp.bfloat16)
+        if d > 0:
+            go(summed.at[at, :], back_got.at[d], b_send.at[d], b_recv.at[d], (g, behind[d], m))
+
+    gates = gate_ref[0].astype(jnp.float32)
+    all_gates = gates[:, 0:1] + gates[:, 1:2]
+    share = (gates[:, 0:1] / all_gates, gates[:, 1:2] / all_gates)
+    routes = route_ref[0]
+    added = jnp.zeros((row_count, quarter), jnp.float32)
+    for d in (0, 1, 3, 2):
+        scale = jnp.where(routes[:, 0:1] == ahead[d], share[0], 0.0)
+        scale = scale + jnp.where(routes[:, 1:2] == ahead[d], share[1], 0.0)
+        if d == 0:
+            came = summed[block(0), :]
+        else:
+            send(back_got.at[d], back_got.at[d], b_send.at[d], b_recv.at[d],
+                 (g, behind[d], m)).wait_recv()
+            came = back_got[d]
+        added = added + scale * came.astype(jnp.float32)
+    own = rows_ref[0, :, cols(m)].astype(jnp.float32) + added
+    moe[:, cols(m)] = own.astype(jnp.bfloat16)
+    for j in (3, 1, 2):
+        go(moe.at[:, cols(m)], moe.at[:, cols(m)], e_send.at[j], e_recv.at[j], (g, e, mp_peer[j]))
+    for j in (1, 2, 3):
+        theirs = moe.at[:, cols(mp_peer[j])]
+        send(theirs, theirs, e_send.at[j], e_recv.at[j], (g, e, mp_peer[j])).wait_recv()
+    loads[2].wait()
+    loads[3].wait()
+    moe_ref[0] = moe[...]
+    encoded = norm_rows(moe[...].astype(jnp.float32), attn_gain_ref[...])
+
+    def kv_copy(d, group, place):
+        return send(kv, kv_got.at[block(d), :], k_send.at[d], k_recv.at[d], (group, place, m))
+
+    @pl.when(g == 0)
+    def _():
+        kv[...] = jnp.dot(encoded, attn[...], preferred_element_type=jnp.float32).astype(
+            jnp.bfloat16
+        )
+        for d in (2, 1, 3, 0):
+            kv_copy(d, 1, ahead[d]).start()
+        step_ref[0] = encoded
+        for d in range(n_expert):
+            kv_copy(d, 1, ahead[d]).wait_send()
+
+    @pl.when(g == 1)
+    def _():
+        query = jnp.dot(
+            encoded, attn[:, 0:head_width], preferred_element_type=jnp.float32
+        ).astype(jnp.bfloat16)
+        positions = cache.shape[0] // row_count
+        lane = lax.broadcasted_iota(jnp.int32, (1, total), 1).astype(jnp.float32)
+        slot = lax.broadcasted_iota(jnp.int32, (row_count, 1), 0).astype(jnp.float32)
+        square = (row_count, row_count)
+        diagonal = lax.broadcasted_iota(jnp.int32, square, 0) == lax.broadcasted_iota(
+            jnp.int32, square, 1
+        )
+        lengths = jnp.sum(
+            jnp.where(diagonal, cache_len_ref[...].astype(jnp.float32), 0.0), axis=1, keepdims=True
+        )
+        cell = jnp.full((1, total), -1.0, jnp.float32)
+        first_slot = (e * row_count).astype(jnp.float32)
+        for d in range(n_expert):
+            facts = meta[d].astype(jnp.float32)
+            start = jnp.full((1, 1), float(d * row_count), jnp.float32)
+            for s in range(src_ref.shape[1]):
+                length = facts[0:1, s : s + 1]
+                place = facts[1:2, s : s + 1] - first_slot
+                here = (lane >= start) & (lane < start + length)
+                cell = jnp.where(here, place * positions + lane - start, cell)
+                lengths = jnp.where(slot == place, length, lengths)
+                start = start + length
+        cell = cell.astype(jnp.int32)
+        for d in range(n_expert):
+            kv_copy(d, 1, ahead[d]).wait_recv()
+
+        def place_cells(c, carry):
+            at = pl.ds(pl.multiple_of(c * tile, tile), tile)
+            spot = lax.broadcasted_iota(jnp.int32, (tile, total), 0) + c * tile
+            hit = jnp.where(spot == cell, 1.0, 0.0)
+            kept = 1.0 - jnp.sum(hit, axis=1, keepdims=True)
+            new = jnp.dot(hit.astype(jnp.bfloat16), kv_got[...], preferred_element_type=jnp.float32)
+            slot_kv[at, :] = (new + kept * cache[at, :].astype(jnp.float32)).astype(jnp.bfloat16)
+            return carry
+
+        lax.fori_loop(0, cache.shape[0] // tile, place_cells, 0)
+        shape = (row_count, cache.shape[0])
+        spot = lax.broadcasted_iota(jnp.int32, shape, 1)
+        offset = spot - positions * lax.broadcasted_iota(jnp.int32, shape, 0)
+        inside = (offset >= 0) & (offset < lengths.astype(jnp.int32))
+        pieces = []
+        for h in range(head_width // HEAD_DIM):
+            low, high = h * HEAD_DIM, (h + 1) * HEAD_DIM
+            scores = lax.dot_general(
+                query[:, low:high], slot_kv[:, low:high], NT, preferred_element_type=jnp.float32
+            ) * (1.0 / math.sqrt(HEAD_DIM))
+            scores = jnp.where(inside, scores, -1e30)
+            highest = jnp.max(scores, axis=-1, keepdims=True)
+            raised = jnp.where(inside, jnp.exp(scores - highest), 0.0)
+            probs = (raised / jnp.sum(raised, axis=-1, keepdims=True)).astype(jnp.bfloat16)
+            pieces.append(
+                jnp.dot(
+                    probs,
+                    slot_kv[:, head_width + low : head_width + high],
+                    preferred_element_type=jnp.float32,
+                ).astype(jnp.bfloat16)
+            )
+        context = jnp.concatenate(pieces, axis=1)
+
+        def mixed_copy(j):
+            return send(mixed.at[j], mixed_got.at[j], g_send.at[j], g_recv.at[j],
+                        (g, e, mp_peer[j]))
+
+        def final_copy(j, place):
+            return send(final.at[:, cols(place)], final.at[:, cols(place)], h_send.at[j],
+                        h_recv.at[j], (g, e, mp_peer[j]))
+
+        for j in (3, 1, 2, 0):
+            mixed[j] = lax.dot_general(
+                context, attn[cols(mp_peer[j]), head_width : 2 * head_width], NT,
+                preferred_element_type=jnp.float32,
+            ).astype(jnp.bfloat16)
+            if j > 0:
+                mixed_copy(j).start()
+        out = mixed[0].astype(jnp.float32)
+        for j in (1, 2, 3):
+            mixed_copy(j).wait_recv()
+            out = out + mixed_got[j].astype(jnp.float32)
+        out = out + moe[:, cols(m)].astype(jnp.float32)
+        final[:, cols(m)] = out.astype(jnp.bfloat16)
+        for j in (3, 1, 2):
+            final_copy(j, m).start()
+        for j in (1, 2, 3):
+            final_copy(j, mp_peer[j]).wait_recv()
+        step_ref[0] = final[...]
+        for j in (1, 2, 3):
+            mixed_copy(j).wait_send()
+            final_copy(j, m).wait_send()
+
+    for copy in pending:
+        copy.wait_send()
+
+
+def dense_body(
+    rows, route, gate_int, moe_gain, w_in, w_out, attn_gain, attn_weight, src_len, target, cache,
+    cache_len,
+):
+    row_count, width = rows.shape[1], rows.shape[2]
+    n_expert = lax.axis_size("expert")
+    total = n_expert * row_count
+    units = w_in.shape[3]
+    quarter = width // 4
+    attn = attn_weight[0].reshape(width, -1)
+    kv_cache = cache.reshape(row_count * cache.shape[1], -1)
+    both = attn.shape[1]
+    bf16 = jnp.bfloat16
+    dma = pltpu.SemaphoreType.DMA
+    vmem = pl.BlockSpec(memory_space=pltpu.VMEM)
+    hbm = pl.BlockSpec(memory_space=pl.ANY)
+    flops = 4 * total * width * units
+    return pl.pallas_call(
+        kernel,
+        out_shape=(jax.ShapeDtypeStruct(rows.shape, bf16), jax.ShapeDtypeStruct(rows.shape, bf16)),
+        in_specs=[vmem] * 8 + [hbm] * 4,
+        out_specs=(vmem, vmem),
+        scratch_shapes=[
+            pltpu.VMEM((width, units), bf16),
+            pltpu.VMEM((units, width), bf16),
+            pltpu.VMEM(attn.shape, bf16),
+            pltpu.VMEM(kv_cache.shape, bf16),
+            pltpu.VMEM((total, width), bf16),
+            pltpu.VMEM((total, units), bf16),
+            pltpu.VMEM((4, total, quarter), bf16),
+            pltpu.VMEM((4, total, quarter), bf16),
+            pltpu.VMEM((total, quarter), bf16),
+            pltpu.VMEM((n_expert, row_count, quarter), bf16),
+            pltpu.VMEM((row_count, width), bf16),
+            pltpu.VMEM((n_expert, 8, 128), jnp.int32),
+            pltpu.VMEM((row_count, both), bf16),
+            pltpu.VMEM((total, both), bf16),
+            pltpu.VMEM(kv_cache.shape, bf16),
+            pltpu.VMEM((4, row_count, quarter), bf16),
+            pltpu.VMEM((4, row_count, quarter), bf16),
+            pltpu.VMEM((row_count, width), bf16),
+            dma((4,)),
+            dma((n_expert,)), dma((n_expert,)),
+            dma((n_expert,)), dma((n_expert,)),
+            dma((n_expert, 4)), dma((n_expert, 4)),
+            dma((4,)), dma((4,)),
+            dma((n_expert,)), dma((n_expert,)),
+            dma((4,)), dma((4,)),
+            dma((n_expert,)), dma((n_expert,)),
+            dma((4,)), dma((4,)),
+            dma((4,)), dma((4,)),
+        ],
+        compiler_params=pltpu.CompilerParams(
+            collective_id=0, has_side_effects=True, vmem_limit_bytes=48 * 1024 * 1024
+        ),
+        cost_estimate=pl.CostEstimate(flops=flops, bytes_accessed=12 << 20, transcendentals=0),
+    )(
+        rows, route, gate_int, moe_gain, attn_gain, src_len, target, cache_len.reshape(1, -1),
+        w_in, w_out, attn, kv_cache,
+    )
+
+
 def solution(mesh):
+    dense = mesh.shape["expert"] == 4 and mesh.shape["mp"] == 4
     return jax.shard_map(
-        body,
+        dense_body if dense else spread_body,
         mesh=mesh,
         in_specs=(
             P("group", "expert", None),

time: 231 us -> 69.4 us (0.30)
  waiting for transfers between devices: 127 us -> 0 us
  Pallas kernels: 0 us -> 61.9 us
  blocking collectives: 33.3 us -> 0 us
  matrix products: 14.6 us -> 0 us
  between operations: 15 us -> 0.75 us
  local copies, waits for them, and re-layouts: 19.8 us -> 6.5 us
  starting transfers between devices: 9.74 us -> 0 us
  other arithmetic: 9.4 us -> 0 us
    psum x2 -> x0, waiting for transfers between devices: 84.2 us -> none  [the longest x1 42.6 us: body(): summed = lax.psum(partial_rows.astype(jnp.bfloat16), 'mp')]
    pallas_call x0 -> x1, Pallas kernels: none -> 61.9 us  [dense_body(): pl.pallas_call(kernel, out_shape=(jax.ShapeDtypeStruct(rows.shape, bf16),...]
    all_to_all x2 -> x0, waiting for transfers between devices: 42.9 us -> none  [the longest x1 25 us: body(): lax.all_to_all(buffer, 'expert', split_axis=0, concat_axis=0, tiled=True)]
    all_gather x1 -> x0, blocking collectives: 25.2 us -> none  [body(): lax.all_gather(projected, ('group', 'expert'), axis=0, tiled=True)]
    dot_general x7 -> x0, matrix products: 14.6 us -> none  [the longest x1 6.79 us: body(): jnp.einsum('scf,fo->sco', hidden, w_out[0, 0], preferred_element_type=jnp...]
    all_to_all x2 -> x0, starting transfers between devices: 9.74 us -> none  [the longest x1 5.42 us: body(): lax.all_to_all(buffer, 'expert', split_axis=0, concat_axis=0, tiled=True)]
    unnamed x1 -> x0, blocking collectives: 8.11 us -> none
    slice x4 -> x0, local copies, waits for them, and re-layouts: 5.93 us -> none  [the longest x1 5.12 us: body(): slot_kv[:, :, 1, :].reshape(row_count, positions, heads_here, HEAD_DIM)]
  transfers between devices with their start and end apart: 4 -> 0, of which waited for: 4 -> 0; matrix products, arithmetic and copies ran while one was open for 4% -> 0% of each run, Pallas kernels for 0% -> 0%
where the time goes in v1:
time: 69.4 us; the launch traced here: 69.1 us
  Pallas kernels  61.9 us (89%)
  local copies, waits for them, and re-layouts  6.5 us (9%)
  between operations  0.75 us (1%)
    pallas_call x1, Pallas kernels, dense_body(): pl.pallas_call(kernel, out_shape=(jax.ShapeDtypeStruct(rows.shape, bf16),...  61.9 us
    unnamed x18, local copies, waits for them, and re-layouts  6.5 us

profile of v1, /device:TPU:1, one launch (start us, length us, event | category | flops | bytes accessed | tf_op | source)
XLA Modules:
  0.0 69.1 jit_solution(4611197450314116943)
XLA Ops:
  0.6 0.0 copy-start.5
  0.6 0.0 copy-start.4
  0.7 0.0 copy-start.3
  0.7 0.0 copy-start.2
  0.7 0.0 copy-start.1
  0.7 0.0 copy-start
  0.7 0.8 %copy.14.route_ref = s32[1,64,2]{2,1,0:T(8,128)S(1)} copy(s32[1,64,2]{1,2,0:T(2,128)} %param.13) | data formatting | bytes 1024 | tf_op args[1]
  1.5 0.8 %copy.15.gate_ref = s32[1,64,2]{2,1,0:T(8,128)S(1)} copy(s32[1,64,2]{1,2,0:T(2,128)} %param.14) | data formatting | bytes 1024 | tf_op args[2]
  2.3 1.4 %copy.17 = bf16[128,8,2,256]{3,1,2,0:T(8,128)(2,1)S(1)} copy(bf16[128,8,2,256]{3,2,1,0:T(2,128)(2,1)} %bitcast.11) | data formatting | bytes 2097152
  3.7 2.0 %copy.16 = bf16[256,8,2,256]{3,1,2,0:T(8,128)(2,1)S(1)} copy(bf16[256,8,2,256]{3,2,1,0:T(2,128)(2,1)} %bitcast.10) | data formatting | bytes 4194304
  5.8 0.0 copy-done.5
  5.8 0.0 copy-done.4
  5.8 0.0 copy-done.3
  5.8 0.0 copy-done.2
  5.8 0.0 copy-done.1
  5.8 0.0 copy-done
  5.8 61.9 %shard_map.131 = (bf16[1,64,2048]{2,1,0:T(8,128)(2,1)S(1)}, bf16[1,64,2048]{2,1,0:T(8,128)(2,1)S(1)}) custom-call(bf16[1,64,2048]{2,1,0:T(8,128)(2,1)S(1)} %copy-done, s32[1,64,2]{2,1,0:T(8,128)S(1)} %copy.14.route_ref, s32[1,64,2]{2,1,0:T(8,128)S(1)} %copy.15.gate_ref, f32[1,2048]{1,0:T(1,128)S(1)} %copy-done.1, f32[1,2048]{1,0:T(1,128)S(1)} %copy-done.2, ...), custom_call_target="tpu_custom_call" | custom-call | flops 2147483648 | bytes 12582912 | tf_op jit(solution)/shard_map/pallas_call | solution.py:418
  67.7 0.7 %copy.20 = bf16[1,64,2048]{2,1,0:T(8,128)(2,1)} copy(bf16[1,64,2048]{2,1,0:T(8,128)(2,1)S(1)} %get-tuple-element.4) | data formatting | bytes 524288
  68.4 0.7 %copy.21 = bf16[1,64,2048]{2,1,0:T(8,128)(2,1)} copy(bf16[1,64,2048]{2,1,0:T(8,128)(2,1)S(1)} %get-tuple-element.5) | data formatting | bytes 524288
Async XLA Ops:
  0.6 5.1 %copy-start.5 = (s32[64]{0:T(128)S(1)}, s32[64]{0:T(128)}, u32[]{:S(2)}) copy-start(s32[64]{0:T(128)} %param.23) | copy-start | bytes 772
  0.6 5.1 %copy-start.4 = (s32[1,6]{1,0:T(1,128)S(1)}, s32[1,6]{1,0:T(1,128)}, u32[]{:S(2)}) copy-start(s32[1,6]{1,0:T(1,128)} %target_ref.1) | copy-start | bytes 76
  0.7 5.1 %copy-start.3 = (s32[1,6]{1,0:T(1,128)S(1)}, s32[1,6]{1,0:T(1,128)}, u32[]{:S(2)}) copy-start(s32[1,6]{1,0:T(1,128)} %src_ref.1) | copy-start | bytes 76
  0.7 5.1 %copy-start.2 = (f32[1,2048]{1,0:T(1,128)S(1)}, f32[1,2048]{1,0:T(1,128)}, u32[]{:S(2)}) copy-start(f32[1,2048]{1,0:T(1,128)} %attn_gain_ref.1) | copy-start | bytes 24580
  0.7 5.1 %copy-start.1 = (f32[1,2048]{1,0:T(1,128)S(1)}, f32[1,2048]{1,0:T(1,128)}, u32[]{:S(2)}) copy-start(f32[1,2048]{1,0:T(1,128)} %moe_gain_ref.1) | copy-start | bytes 24580
  0.7 5.1 %copy-start = (bf16[1,64,2048]{2,1,0:T(8,128)(2,1)S(1)}, bf16[1,64,2048]{2,1,0:T(8,128)(2,1)}, u32[]{:S(2)}) copy-start(bf16[1,64,2048]{2,1,0:T(8,128)(2,1)} %rows_ref.1) | copy-start | bytes 786436

commit v2 on v1

--- a/solution.py
+++ b/solution.py
@@ -150,10 +150,10 @@
 
 def kernel(
     rows_ref, route_ref, gate_ref, moe_gain_ref, attn_gain_ref, src_ref, target_ref, cache_len_ref,
-    w_in_hbm, w_out_hbm, attn_hbm, cache_hbm,
+    attn, cache, w_in_hbm, w_out_hbm,
     moe_ref, step_ref,
-    w_in, w_out, attn, cache, gathered, hidden, part, part_got, summed, back_got, moe, meta,
-    kv, kv_got, slot_kv, mixed, mixed_got, final,
+    w_in, w_out, gathered, hidden, part, part_got, summed, back_got, moe, meta,
+    kv, kv_got, mixed, mixed_got, final,
     load_sem, z_send, z_recv, m_send, m_recv, f_send, f_recv, p_send, p_recv, b_send, b_recv,
     e_send, e_recv, k_send, k_recv, g_send, g_recv, h_send, h_recv,
 ):
@@ -174,8 +174,6 @@
     loads = [
         pltpu.make_async_copy(w_in_hbm.at[0, 0], w_in, load_sem.at[0]),
         pltpu.make_async_copy(w_out_hbm.at[0, 0], w_out, load_sem.at[1]),
-        pltpu.make_async_copy(attn_hbm, attn, load_sem.at[2]),
-        pltpu.make_async_copy(cache_hbm, cache, load_sem.at[3]),
     ]
     barrier = pltpu.get_barrier_semaphore()
     friends = [(g, ahead[d], m) for d in range(1, n_expert)]
@@ -189,8 +187,18 @@
     def cols(place):
         return pl.ds(pl.multiple_of(place * quarter, quarter), quarter)
 
+    order = (0, 1, 3, 2)
+    spans = ((0, 1), (1, 3), (3, 4))
+
     def block(d):
+        return pl.ds(order.index(d) * row_count, row_count)
+
+    def kv_block(d):
         return pl.ds(d * row_count, row_count)
+
+    def span(k):
+        low, high = spans[k]
+        return pl.ds(low * row_count, (high - low) * row_count)
 
     def send(src, dst, send_sem, recv_sem, device):
         copy = pltpu.make_async_remote_copy(
@@ -213,60 +221,98 @@
     meta[0, 1:2, 0:src_ref.shape[1]] = target_ref[...]
     pl.semaphore_wait(barrier, len(friends))
 
-    for d in (2, 1, 3):
-        go(gathered.at[block(0), cols(m)], gathered.at[block(d), cols(m)],
-           z_send.at[d], z_recv.at[d], (g, ahead[d], m))
-    for d in (1, 2, 3):
-        go(meta.at[0], meta.at[d], m_send.at[d], m_recv.at[d], (g, ahead[d], m))
-    for d in (1, 3, 2):
+    def z_copy(d):
+        return send(gathered.at[block(0), cols(m)], gathered.at[block(d), cols(m)],
+                    z_send.at[d], z_recv.at[d], (g, ahead[d], m))
+
+    def forward(d):
         mine = gathered.at[block(d), cols(m)]
-        send(mine, mine, z_send.at[d], z_recv.at[d], (g, ahead[d], m)).wait_recv()
+        z_copy(d).wait_recv()
         for j in (3, 1, 2):
             go(mine, mine, f_send.at[d, j], f_recv.at[d, j], (g, e, mp_peer[j]))
-    for d in (1, 2, 3):
-        send(meta.at[d], meta.at[d], m_send.at[d], m_recv.at[d], (g, ahead[d], m)).wait_recv()
-    for d in (1, 3, 2):
+
+    def forwarded(d):
         for j in (1, 2, 3):
             theirs = gathered.at[block(d), cols(mp_peer[j])]
             send(theirs, theirs, f_send.at[d, j], f_recv.at[d, j], (g, e, mp_peer[j])).wait_recv()
 
+    tile = 256
+
+    def first_product(k):
+        def step(n, carry):
+            at = pl.ds(pl.multiple_of(n * tile, tile), tile)
+            raw = jnp.dot(gathered[span(k), :], w_in[:, at], preferred_element_type=jnp.float32)
+            hidden[span(k), at] = jnp.maximum(raw, 0.0).astype(jnp.bfloat16)
+            return carry
+
+        lax.fori_loop(0, w_in.shape[1] // tile, step, 0)
+
+    def part_copy(k, j):
+        return send(part.at[j, span(k), :], part_got.at[j, span(k), :], p_send.at[k, j],
+                    p_recv.at[k, j], (g, e, mp_peer[j]))
+
+    def second_product(k):
+        for j in (3, 1, 2, 0):
+            part[j, span(k), :] = jnp.dot(
+                hidden[span(k), :], w_out[:, cols(mp_peer[j])], preferred_element_type=jnp.float32
+            ).astype(jnp.bfloat16)
+            if j > 0:
+                pending.append(part_copy(k, j))
+                pending[-1].start()
+
+    def add_parts(k):
+        for j in (1, 2, 3):
+            part_copy(k, j).wait_recv()
+        for d in order[spans[k][0] : spans[k][1]]:
+            at = block(d)
+            whole = part[0, at, :].astype(jnp.float32)
+            for j in (1, 2, 3):
+                whole = whole + part_got[j, at, :].astype(jnp.float32)
+            summed[at, :] = whole.astype(jnp.bfloat16)
+            if d > 0:
+                go(summed.at[at, :], back_got.at[d], b_send.at[d], b_recv.at[d], (g, behind[d], m))
+
+    for d in (1, 3, 2):
+        pending.append(z_copy(d))
+        pending[-1].start()
+    for d in (1, 2, 3):
+        go(meta.at[0], meta.at[d], m_send.at[d], m_recv.at[d], (g, ahead[d], m))
     loads[0].wait()
-    tile = 256
-
-    def first(n, carry):
-        at = pl.ds(pl.multiple_of(n * tile, tile), tile)
-        raw = jnp.dot(gathered[...], w_in[:, at], preferred_element_type=jnp.float32)
-        hidden[:, at] = jnp.maximum(raw, 0.0).astype(jnp.bfloat16)
-        return carry
-
-    lax.fori_loop(0, w_in.shape[1] // tile, first, 0)
-
+    first_product(0)
+    forward(1)
+    forward(3)
     loads[1].wait()
-    for j in (3, 1, 2, 0):
-        part[j] = jnp.dot(
-            hidden[...], w_out[:, cols(mp_peer[j])], preferred_element_type=jnp.float32
-        ).astype(jnp.bfloat16)
-        if j > 0:
-            go(part.at[j], part_got.at[j], p_send.at[j], p_recv.at[j], (g, e, mp_peer[j]))
-    for j in (1, 2, 3):
-        send(part.at[j], part_got.at[j], p_send.at[j], p_recv.at[j], (g, e, mp_peer[j])).wait_recv()
-    for d in (2, 1, 3, 0):
-        at = block(d)
-        whole = part[0, at, :].astype(jnp.float32)
-        for j in (1, 2, 3):
-            whole = whole + part_got[j, at, :].astype(jnp.float32)
-        summed[at, :] = whole.astype(jnp.bfloat16)
-        if d > 0:
-            go(summed.at[at, :], back_got.at[d], b_send.at[d], b_recv.at[d], (g, behind[d], m))
-
-    gates = gate_ref[0].astype(jnp.float32)
-    all_gates = gates[:, 0:1] + gates[:, 1:2]
-    share = (gates[:, 0:1] / all_gates, gates[:, 1:2] / all_gates)
-    routes = route_ref[0]
+    second_product(0)
+    forward(2)
+    forwarded(1)
+    forwarded(3)
+    first_product(1)
+    second_product(1)
+    forwarded(2)
+    first_product(2)
+    second_product(2)
+    add_parts(0)
+    add_parts(1)
+    add_parts(2)
+
+    square = (row_count, row_count)
+    diagonal = lax.broadcasted_iota(jnp.int32, square, 0) == lax.broadcasted_iota(
+        jnp.int32, square, 1
+    )
+
+    def upright(line):
+        return jnp.sum(jnp.where(diagonal, line.astype(jnp.float32), 0.0), axis=1, keepdims=True)
+
+    gates = [upright(gate_ref[0, k : k + 1, :]) for k in (0, 1)]
+    routes = [upright(route_ref[0, k : k + 1, :]) for k in (0, 1)]
+    share = [gate / (gates[0] + gates[1]) for gate in gates]
+    for d in (1, 2, 3):
+        send(meta.at[d], meta.at[d], m_send.at[d], m_recv.at[d], (g, ahead[d], m)).wait_recv()
     added = jnp.zeros((row_count, quarter), jnp.float32)
     for d in (0, 1, 3, 2):
-        scale = jnp.where(routes[:, 0:1] == ahead[d], share[0], 0.0)
-        scale = scale + jnp.where(routes[:, 1:2] == ahead[d], share[1], 0.0)
+        expert = ahead[d].astype(jnp.float32)
+        scale = jnp.where(routes[0] == expert, share[0], 0.0)
+        scale = scale + jnp.where(routes[1] == expert, share[1], 0.0)
         if d == 0:
             came = summed[block(0), :]
         else:
@@ -281,13 +327,11 @@
     for j in (1, 2, 3):
         theirs = moe.at[:, cols(mp_peer[j])]
         send(theirs, theirs, e_send.at[j], e_recv.at[j], (g, e, mp_peer[j])).wait_recv()
-    loads[2].wait()
-    loads[3].wait()
     moe_ref[0] = moe[...]
     encoded = norm_rows(moe[...].astype(jnp.float32), attn_gain_ref[...])
 
     def kv_copy(d, group, place):
-        return send(kv, kv_got.at[block(d), :], k_send.at[d], k_recv.at[d], (group, place, m))
+        return send(kv, kv_got.at[kv_block(d), :], k_send.at[d], k_recv.at[d], (group, place, m))
 
     @pl.when(g == 0)
     def _():
@@ -308,14 +352,8 @@
         positions = cache.shape[0] // row_count
         lane = lax.broadcasted_iota(jnp.int32, (1, total), 1).astype(jnp.float32)
         slot = lax.broadcasted_iota(jnp.int32, (row_count, 1), 0).astype(jnp.float32)
-        square = (row_count, row_count)
-        diagonal = lax.broadcasted_iota(jnp.int32, square, 0) == lax.broadcasted_iota(
-            jnp.int32, square, 1
-        )
-        lengths = jnp.sum(
-            jnp.where(diagonal, cache_len_ref[...].astype(jnp.float32), 0.0), axis=1, keepdims=True
-        )
-        cell = jnp.full((1, total), -1.0, jnp.float32)
+        lengths = upright(cache_len_ref[...])
+        row_slot = jnp.full((1, total), -1.0, jnp.float32)
         first_slot = (e * row_count).astype(jnp.float32)
         for d in range(n_expert):
             facts = meta[d].astype(jnp.float32)
@@ -324,44 +362,36 @@
                 length = facts[0:1, s : s + 1]
                 place = facts[1:2, s : s + 1] - first_slot
                 here = (lane >= start) & (lane < start + length)
-                cell = jnp.where(here, place * positions + lane - start, cell)
-                lengths = jnp.where(slot == place, length, lengths)
+                row_slot = jnp.where(here, place, row_slot)
+                lengths = jnp.where(slot == place, 0.0, lengths)
                 start = start + length
-        cell = cell.astype(jnp.int32)
-        for d in range(n_expert):
-            kv_copy(d, 1, ahead[d]).wait_recv()
-
-        def place_cells(c, carry):
-            at = pl.ds(pl.multiple_of(c * tile, tile), tile)
-            spot = lax.broadcasted_iota(jnp.int32, (tile, total), 0) + c * tile
-            hit = jnp.where(spot == cell, 1.0, 0.0)
-            kept = 1.0 - jnp.sum(hit, axis=1, keepdims=True)
-            new = jnp.dot(hit.astype(jnp.bfloat16), kv_got[...], preferred_element_type=jnp.float32)
-            slot_kv[at, :] = (new + kept * cache[at, :].astype(jnp.float32)).astype(jnp.bfloat16)
-            return carry
-
-        lax.fori_loop(0, cache.shape[0] // tile, place_cells, 0)
         shape = (row_count, cache.shape[0])
-        spot = lax.broadcasted_iota(jnp.int32, shape, 1)
-        offset = spot - positions * lax.broadcasted_iota(jnp.int32, shape, 0)
-        inside = (offset >= 0) & (offset < lengths.astype(jnp.int32))
-        pieces = []
-        for h in range(head_width // HEAD_DIM):
+        offset = lax.broadcasted_iota(
+            jnp.int32, shape, 1
+        ) - positions * lax.broadcasted_iota(jnp.int32, shape, 0)
+        held = (offset >= 0) & (offset < lengths.astype(jnp.int32))
+        fresh = slot == row_slot
+
+        def attend(h, pool, inside):
             low, high = h * HEAD_DIM, (h + 1) * HEAD_DIM
             scores = lax.dot_general(
-                query[:, low:high], slot_kv[:, low:high], NT, preferred_element_type=jnp.float32
+                query[:, low:high], pool[:, low:high], NT, preferred_element_type=jnp.float32
             ) * (1.0 / math.sqrt(HEAD_DIM))
             scores = jnp.where(inside, scores, -1e30)
             highest = jnp.max(scores, axis=-1, keepdims=True)
             raised = jnp.where(inside, jnp.exp(scores - highest), 0.0)
-            probs = (raised / jnp.sum(raised, axis=-1, keepdims=True)).astype(jnp.bfloat16)
-            pieces.append(
-                jnp.dot(
-                    probs,
-                    slot_kv[:, head_width + low : head_width + high],
-                    preferred_element_type=jnp.float32,
-                ).astype(jnp.bfloat16)
+            weight = jnp.sum(raised, axis=-1, keepdims=True)
+            probs = (raised / jnp.where(weight > 0.0, weight, 1.0)).astype(jnp.bfloat16)
+            return jnp.dot(
+                probs, pool[:, head_width + low : head_width + high],
+                preferred_element_type=jnp.float32,
             )
+
+        heads = range(head_width // HEAD_DIM)
+        from_cache = [attend(h, cache, held) for h in heads]
+        for d in range(n_expert):
+            kv_copy(d, 1, ahead[d]).wait_recv()
+        pieces = [(from_cache[h] + attend(h, kv_got, fresh)).astype(jnp.bfloat16) for h in heads]
         context = jnp.concatenate(pieces, axis=1)
 
         def mixed_copy(j):
@@ -418,13 +448,11 @@
     return pl.pallas_call(
         kernel,
         out_shape=(jax.ShapeDtypeStruct(rows.shape, bf16), jax.ShapeDtypeStruct(rows.shape, bf16)),
-        in_specs=[vmem] * 8 + [hbm] * 4,
+        in_specs=[vmem] * 10 + [hbm] * 2,
         out_specs=(vmem, vmem),
         scratch_shapes=[
             pltpu.VMEM((width, units), bf16),
             pltpu.VMEM((units, width), bf16),
-            pltpu.VMEM(attn.shape, bf16),
-            pltpu.VMEM(kv_cache.shape, bf16),
             pltpu.VMEM((total, width), bf16),
             pltpu.VMEM((total, units), bf16),
             pltpu.VMEM((4, total, quarter), bf16),
@@ -435,15 +463,14 @@
             pltpu.VMEM((n_expert, 8, 128), jnp.int32),
             pltpu.VMEM((row_count, both), bf16),
             pltpu.VMEM((total, both), bf16),
-            pltpu.VMEM(kv_cache.shape, bf16),
             pltpu.VMEM((4, row_count, quarter), bf16),
             pltpu.VMEM((4, row_count, quarter), bf16),
             pltpu.VMEM((row_count, width), bf16),
-            dma((4,)),
+            dma((2,)),
             dma((n_expert,)), dma((n_expert,)),
             dma((n_expert,)), dma((n_expert,)),
             dma((n_expert, 4)), dma((n_expert, 4)),
-            dma((4,)), dma((4,)),
+            dma((3, 4)), dma((3, 4)),
             dma((n_expert,)), dma((n_expert,)),
             dma((4,)), dma((4,)),
             dma((n_expert,)), dma((n_expert,)),
@@ -455,8 +482,8 @@
         ),
         cost_estimate=pl.CostEstimate(flops=flops, bytes_accessed=12 << 20, transcendentals=0),
     )(
-        rows, route, gate_int, moe_gain, attn_gain, src_len, target, cache_len.reshape(1, -1),
-        w_in, w_out, attn, kv_cache,
+        rows, route.transpose(0, 2, 1), gate_int.transpose(0, 2, 1), moe_gain, attn_gain, src_len,
+        target, cache_len.reshape(1, -1), attn, kv_cache, w_in, w_out,
     )
 
 

time: 69.4 us -> 59.4 us (0.86)
  Pallas kernels: 61.9 us -> 53.5 us
  local copies, waits for them, and re-layouts: 6.5 us -> 4.97 us
    pallas_call x1, Pallas kernels: 61.9 us -> 53.5 us  [dense_body(): pl.pallas_call(kernel, out_shape=(jax.ShapeDtypeStruct(rows.shape, bf16),...]
    unnamed x18 -> x20, local copies, waits for them, and re-layouts: 6.5 us -> 4.97 us
where the time goes in v2:
time: 59.4 us; the launch traced here: 59.2 us
  Pallas kernels  53.5 us (90%)
  local copies, waits for them, and re-layouts  4.97 us (8%)
  between operations  0.78 us (1%)
    pallas_call x1, Pallas kernels, dense_body(): pl.pallas_call(kernel, out_shape=(jax.ShapeDtypeStruct(rows.shape, bf16),...  53.5 us
    unnamed x20, local copies, waits for them, and re-layouts  4.97 us

profile of v2, /device:TPU:1, one launch (start us, length us, event | category | flops | bytes accessed | tf_op | source)
XLA Modules:
  0.0 59.2 jit_solution(13462337442801249812)
XLA Ops:
  0.6 0.0 copy-start.7
  0.6 0.0 copy-start.6
  0.7 0.0 copy-start.5
  0.7 0.0 copy-start.2
  0.7 0.0 copy-start.1
  0.7 0.0 copy-start.4
  0.7 0.0 copy-start.3
  0.7 0.0 copy-start
  0.7 1.5 %copy.15 = bf16[128,8,2,256]{3,1,2,0:T(8,128)(2,1)S(1)} copy(bf16[128,8,2,256]{3,2,1,0:T(2,128)(2,1)} %bitcast.15) | data formatting | bytes 2097152
  2.2 2.0 %copy.14 = bf16[256,8,2,256]{3,1,2,0:T(8,128)(2,1)S(1)} copy(bf16[256,8,2,256]{3,2,1,0:T(2,128)(2,1)} %bitcast.14) | data formatting | bytes 4194304
  4.3 0.0 copy-done.7
  4.3 0.0 copy-done.6
  4.3 0.0 copy-done.5
  4.3 0.0 copy-done.2
  4.3 0.0 copy-done.1
  4.3 0.0 copy-done.4
  4.3 0.0 copy-done.3
  4.3 0.0 copy-done
  4.3 53.5 %shard_map.131 = (bf16[1,64,2048]{2,1,0:T(8,128)(2,1)S(1)}, bf16[1,64,2048]{2,1,0:T(8,128)(2,1)S(1)}) custom-call(bf16[1,64,2048]{2,1,0:T(8,128)(2,1)S(1)} %copy-done, s32[1,2,64]{2,1,0:T(2,128)S(1)} %bitcast.11, s32[1,2,64]{2,1,0:T(2,128)S(1)} %bitcast.12, f32[1,2048]{1,0:T(1,128)S(1)} %copy-done.1, f32[1,2048]{1,0:T(1,128)S(1)} %copy-done.2, ...), custom_call_target="tpu_custom_call" | custom-call | flops 2147483648 | bytes 12582912 | tf_op jit(solution)/shard_map/pallas_call | solution.py:448
  57.8 0.7 %copy.18 = bf16[1,64,2048]{2,1,0:T(8,128)(2,1)} copy(bf16[1,64,2048]{2,1,0:T(8,128)(2,1)S(1)} %get-tuple-element.4) | data formatting | bytes 524288
  58.5 0.7 %copy.19 = bf16[1,64,2048]{2,1,0:T(8,128)(2,1)} copy(bf16[1,64,2048]{2,1,0:T(8,128)(2,1)S(1)} %get-tuple-element.5) | data formatting | bytes 524288
Async XLA Ops:
  0.6 3.6 %copy-start.7 = (s32[64]{0:T(128)S(1)}, s32[64]{0:T(128)}, u32[]{:S(2)}) copy-start(s32[64]{0:T(128)} %param.23) | copy-start | bytes 772
  0.6 3.6 %copy-start.6 = (s32[1,6]{1,0:T(1,128)S(1)}, s32[1,6]{1,0:T(1,128)}, u32[]{:S(2)}) copy-start(s32[1,6]{1,0:T(1,128)} %target_ref.1) | copy-start | bytes 76
  0.7 3.6 %copy-start.5 = (s32[1,6]{1,0:T(1,128)S(1)}, s32[1,6]{1,0:T(1,128)}, u32[]{:S(2)}) copy-start(s32[1,6]{1,0:T(1,128)} %src_ref.1) | copy-start | bytes 76
  0.7 3.6 %copy-start.2 = (f32[1,2048]{1,0:T(1,128)S(1)}, f32[1,2048]{1,0:T(1,128)}, u32[]{:S(2)}) copy-start(f32[1,2048]{1,0:T(1,128)} %attn_gain_ref.1) | copy-start | bytes 24580
  0.7 3.6 %copy-start.1 = (f32[1,2048]{1,0:T(1,128)S(1)}, f32[1,2048]{1,0:T(1,128)}, u32[]{:S(2)}) copy-start(f32[1,2048]{1,0:T(1,128)} %moe_gain_ref.1) | copy-start | bytes 24580
  0.7 3.6 %copy-start.4 = (s32[1,64,2]{1,2,0:T(2,128)S(1)}, s32[1,64,2]{1,2,0:T(2,128)}, u32[]{:S(2)}) copy-start(s32[1,64,2]{1,2,0:T(2,128)} %param.14) | copy-start | bytes 1540
  0.7 3.6 %copy-start.3 = (s32[1,64,2]{1,2,0:T(2,128)S(1)}, s32[1,64,2]{1,2,0:T(2,128)}, u32[]{:S(2)}) copy-start(s32[1,64,2]{1,2,0:T(2,128)} %param.13) | copy-start | bytes 1540
  0.7 3.6 %copy-start = (bf16[1,64,2048]{2,1,0:T(8,128)(2,1)S(1)}, bf16[1,64,2048]{2,1,0:T(8,128)(2,1)}, u32[]{:S(2)}) copy-start(bf16[1,64,2048]{2,1,0:T(8,128)(2,1)} %rows_ref.1) | copy-start | bytes 786436

commit v3 on v2

--- a/solution.py
+++ b/solution.py
@@ -150,9 +150,9 @@
 
 def kernel(
     rows_ref, route_ref, gate_ref, moe_gain_ref, attn_gain_ref, src_ref, target_ref, cache_len_ref,
-    attn, cache, w_in_hbm, w_out_hbm,
+    w_in_hbm, w_out_hbm, attn_hbm, cache_hbm,
     moe_ref, step_ref,
-    w_in, w_out, gathered, hidden, part, part_got, summed, back_got, moe, meta,
+    attn_pairs, cache_pairs, attn, cache, w_in, w_out, gathered, hidden, part, part_got, summed, back_got, moe, meta,
     kv, kv_got, mixed, mixed_got, final,
     load_sem, z_send, z_recv, m_send, m_recv, f_send, f_recv, p_send, p_recv, b_send, b_recv,
     e_send, e_recv, k_send, k_recv, g_send, g_recv, h_send, h_recv,
@@ -174,6 +174,8 @@
     loads = [
         pltpu.make_async_copy(w_in_hbm.at[0, 0], w_in, load_sem.at[0]),
         pltpu.make_async_copy(w_out_hbm.at[0, 0], w_out, load_sem.at[1]),
+        pltpu.make_async_copy(attn_hbm, attn_pairs, load_sem.at[2]),
+        pltpu.make_async_copy(cache_hbm, cache_pairs, load_sem.at[3]),
     ]
     barrier = pltpu.get_barrier_semaphore()
     friends = [(g, ahead[d], m) for d in range(1, n_expert)]
@@ -271,6 +273,17 @@
             summed[at, :] = whole.astype(jnp.bfloat16)
             if d > 0:
                 go(summed.at[at, :], back_got.at[d], b_send.at[d], b_recv.at[d], (g, behind[d], m))
+
+    def planes(pairs, flat, low, high):
+        rows_at_once = 64
+
+        def step(i, carry):
+            at = pl.ds(pl.multiple_of(i * rows_at_once, rows_at_once), rows_at_once)
+            for plane in (0, 1):
+                flat[at, plane * head_width : (plane + 1) * head_width] = pairs[at, plane, :]
+            return carry
+
+        lax.fori_loop(low // rows_at_once, high // rows_at_once, step, 0)
 
     for d in (1, 3, 2):
         pending.append(z_copy(d))
@@ -284,16 +297,20 @@
     loads[1].wait()
     second_product(0)
     forward(2)
+    loads[2].wait()
+    planes(attn_pairs, attn, 0, width // 2)
     forwarded(1)
     forwarded(3)
     first_product(1)
+    add_parts(0)
     second_product(1)
     forwarded(2)
     first_product(2)
     second_product(2)
-    add_parts(0)
     add_parts(1)
+    planes(attn_pairs, attn, width // 2, 3 * width // 4)
     add_parts(2)
+    planes(attn_pairs, attn, 3 * width // 4, width)
 
     square = (row_count, row_count)
     diagonal = lax.broadcasted_iota(jnp.int32, square, 0) == lax.broadcasted_iota(
@@ -324,6 +341,12 @@
     moe[:, cols(m)] = own.astype(jnp.bfloat16)
     for j in (3, 1, 2):
         go(moe.at[:, cols(m)], moe.at[:, cols(m)], e_send.at[j], e_recv.at[j], (g, e, mp_peer[j]))
+    loads[3].wait()
+
+    @pl.when(g == 1)
+    def _():
+        planes(cache_pairs, cache, 0, cache.shape[0])
+
     for j in (1, 2, 3):
         theirs = moe.at[:, cols(mp_peer[j])]
         send(theirs, theirs, e_send.at[j], e_recv.at[j], (g, e, mp_peer[j])).wait_recv()
@@ -437,9 +460,9 @@
     total = n_expert * row_count
     units = w_in.shape[3]
     quarter = width // 4
-    attn = attn_weight[0].reshape(width, -1)
-    kv_cache = cache.reshape(row_count * cache.shape[1], -1)
-    both = attn.shape[1]
+    attn = attn_weight[0]
+    kv_cache = cache.reshape(row_count * cache.shape[1], 2, -1)
+    both = 2 * attn.shape[2]
     bf16 = jnp.bfloat16
     dma = pltpu.SemaphoreType.DMA
     vmem = pl.BlockSpec(memory_space=pltpu.VMEM)
@@ -448,9 +471,13 @@
     return pl.pallas_call(
         kernel,
         out_shape=(jax.ShapeDtypeStruct(rows.shape, bf16), jax.ShapeDtypeStruct(rows.shape, bf16)),
-        in_specs=[vmem] * 10 + [hbm] * 2,
+        in_specs=[vmem] * 8 + [hbm] * 4,
         out_specs=(vmem, vmem),
         scratch_shapes=[
+            pltpu.VMEM(attn.shape, bf16),
+            pltpu.VMEM(kv_cache.shape, bf16),
+            pltpu.VMEM((width, both), bf16),
+            pltpu.VMEM((kv_cache.shape[0], both), bf16),
             pltpu.VMEM((width, units), bf16),
             pltpu.VMEM((units, width), bf16),
             pltpu.VMEM((total, width), bf16),
@@ -466,7 +493,7 @@
             pltpu.VMEM((4, row_count, quarter), bf16),
             pltpu.VMEM((4, row_count, quarter), bf16),
             pltpu.VMEM((row_count, width), bf16),
-            dma((2,)),
+            dma((4,)),
             dma((n_expert,)), dma((n_expert,)),
             dma((n_expert,)), dma((n_expert,)),
             dma((n_expert, 4)), dma((n_expert, 4)),
@@ -483,7 +510,7 @@
         cost_estimate=pl.CostEstimate(flops=flops, bytes_accessed=12 << 20, transcendentals=0),
     )(
         rows, route.transpose(0, 2, 1), gate_int.transpose(0, 2, 1), moe_gain, attn_gain, src_len,
-        target, cache_len.reshape(1, -1), attn, kv_cache, w_in, w_out,
+        target, cache_len.reshape(1, -1), w_in, w_out, attn, kv_cache,
     )
 
 

time: 59.4 us -> 64.1 us (1.079)
  local copies, waits for them, and re-layouts: 4.97 us -> 9.88 us
    unnamed x20 -> x22, local copies, waits for them, and re-layouts: 4.97 us -> 9.88 us
where the time goes in v3:
time: 64.1 us; the launch traced here: 63.7 us
  Pallas kernels  53.2 us (83%)
  local copies, waits for them, and re-layouts  9.88 us (15%)
  between operations  0.66 us (1%)
    pallas_call x1, Pallas kernels, dense_body(): pl.pallas_call(kernel, out_shape=(jax.ShapeDtypeStruct(rows.shape, bf16),...  53.2 us
    unnamed x22, local copies, waits for them, and re-layouts  9.88 us

profile of v3, /device:TPU:1, one launch (start us, length us, event | category | flops | bytes accessed | tf_op | source)
XLA Modules:
  0.0 63.7 jit_solution(16571218390943206100)
XLA Ops:
  0.6 0.0 copy-start
  0.6 1.6 %copy-done = bf16[1,2048,2,256]{3,2,1,0:T(2,128)(2,1)S(1)} copy-done((bf16[1,2048,2,256]{3,2,1,0:T(2,128)(2,1)S(1)}, bf16[1,2048,2,256]{3,2,1,0:T(2,128)(2,1)}, u32[]{:S(2)}) %copy-start) | copy-done | bytes 2097176
  2.2 0.0 copy-start.1
  2.2 1.2 %copy-done.1 = bf16[64,16,2,256]{3,2,1,0:T(2,128)(2,1)S(1)} copy-done((bf16[64,16,2,256]{3,2,1,0:T(2,128)(2,1)S(1)}, bf16[64,16,2,256]{3,2,1,0:T(2,128)(2,1)}, u32[]{:S(2)}) %copy-start.1) | copy-done | bytes 1048600
  3.5 0.0 copy-start.2
  3.5 0.9 %copy-done.2 = bf16[1,64,2048]{2,1,0:T(8,128)(2,1)S(1)} copy-done((bf16[1,64,2048]{2,1,0:T(8,128)(2,1)S(1)}, bf16[1,64,2048]{2,1,0:T(8,128)(2,1)}, u32[]{:S(2)}) %copy-start.2) | copy-done | bytes 262168
  4.4 0.0 copy-start.3
  4.4 0.7 %copy-done.3 = f32[1,2048]{1,0:T(1,128)S(1)} copy-done((f32[1,2048]{1,0:T(1,128)S(1)}, f32[1,2048]{1,0:T(1,128)}, u32[]{:S(2)}) %copy-start.3) | copy-done | bytes 8216
  5.1 0.0 copy-start.4
  5.1 0.7 %copy-done.4 = f32[1,2048]{1,0:T(1,128)S(1)} copy-done((f32[1,2048]{1,0:T(1,128)S(1)}, f32[1,2048]{1,0:T(1,128)}, u32[]{:S(2)}) %copy-start.4) | copy-done | bytes 8216
  5.8 0.0 copy-start.5
  5.8 0.7 %copy-done.5 = s32[1,64,2]{1,2,0:T(2,128)S(1)} copy-done((s32[1,64,2]{1,2,0:T(2,128)S(1)}, s32[1,64,2]{1,2,0:T(2,128)}, u32[]{:S(2)}) %copy-start.5) | copy-done | bytes 536
  6.5 0.0 copy-start.6
  6.5 0.7 %copy-done.6 = s32[1,64,2]{1,2,0:T(2,128)S(1)} copy-done((s32[1,64,2]{1,2,0:T(2,128)S(1)}, s32[1,64,2]{1,2,0:T(2,128)}, u32[]{:S(2)}) %copy-start.6) | copy-done | bytes 536
  7.2 0.0 copy-start.7
  7.2 0.7 %copy-done.7 = s32[1,6]{1,0:T(1,128)S(1)} copy-done((s32[1,6]{1,0:T(1,128)S(1)}, s32[1,6]{1,0:T(1,128)}, u32[]{:S(2)}) %copy-start.7) | copy-done | bytes 48
  7.8 0.0 copy-start.8
  7.8 0.7 %copy-done.8 = s32[1,6]{1,0:T(1,128)S(1)} copy-done((s32[1,6]{1,0:T(1,128)S(1)}, s32[1,6]{1,0:T(1,128)}, u32[]{:S(2)}) %copy-start.8) | copy-done | bytes 48
  8.5 0.0 copy-start.9
  8.5 0.7 %copy-done.9 = s32[64]{0:T(128)S(1)} copy-done((s32[64]{0:T(128)S(1)}, s32[64]{0:T(128)}, u32[]{:S(2)}) %copy-start.9) | copy-done | bytes 280
  9.1 53.2 %shard_map.131 = (bf16[1,64,2048]{2,1,0:T(8,128)(2,1)S(1)}, bf16[1,64,2048]{2,1,0:T(8,128)(2,1)S(1)}) custom-call(bf16[1,64,2048]{2,1,0:T(8,128)(2,1)S(1)} %copy-done.2, s32[1,2,64]{2,1,0:T(2,128)S(1)} %bitcast.7, s32[1,2,64]{2,1,0:T(2,128)S(1)} %bitcast.8, f32[1,2048]{1,0:T(1,128)S(1)} %copy-done.3, f32[1,2048]{1,0:T(1,128)S(1)} %copy-done.4, ...), custom_call_target="tpu_custom_call" | custom-call | flops 2147483648 | bytes 12582912 | tf_op jit(solution)/shard_map/pallas_call | solution.py:471
  62.3 0.7 %copy.16 = bf16[1,64,2048]{2,1,0:T(8,128)(2,1)} copy(bf16[1,64,2048]{2,1,0:T(8,128)(2,1)S(1)} %get-tuple-element.4) | data formatting | bytes 524288
  63.0 0.7 %copy.17 = bf16[1,64,2048]{2,1,0:T(8,128)(2,1)} copy(bf16[1,64,2048]{2,1,0:T(8,128)(2,1)S(1)} %get-tuple-element.5) | data formatting | bytes 524288
Async XLA Ops:
  0.6 1.6 %copy-start = (bf16[1,2048,2,256]{3,2,1,0:T(2,128)(2,1)S(1)}, bf16[1,2048,2,256]{3,2,1,0:T(2,128)(2,1)}, u32[]{:S(2)}) copy-start(bf16[1,2048,2,256]{3,2,1,0:T(2,128)(2,1)} %param.19) | copy-start | bytes 6291460
  2.2 1.2 %copy-start.1 = (bf16[64,16,2,256]{3,2,1,0:T(2,128)(2,1)S(1)}, bf16[64,16,2,256]{3,2,1,0:T(2,128)(2,1)}, u32[]{:S(2)}) copy-start(bf16[64,16,2,256]{3,2,1,0:T(2,128)(2,1)} %param.22) | copy-start | bytes 3145732
  3.5 0.9 %copy-start.2 = (bf16[1,64,2048]{2,1,0:T(8,128)(2,1)S(1)}, bf16[1,64,2048]{2,1,0:T(8,128)(2,1)}, u32[]{:S(2)}) copy-start(bf16[1,64,2048]{2,1,0:T(8,128)(2,1)} %rows_ref.1) | copy-start | bytes 786436
  4.4 0.7 %copy-start.3 = (f32[1,2048]{1,0:T(1,128)S(1)}, f32[1,2048]{1,0:T(1,128)}, u32[]{:S(2)}) copy-start(f32[1,2048]{1,0:T(1,128)} %moe_gain_ref.1) | copy-start | bytes 24580
  5.1 0.7 %copy-start.4 = (f32[1,2048]{1,0:T(1,128)S(1)}, f32[1,2048]{1,0:T(1,128)}, u32[]{:S(2)}) copy-start(f32[1,2048]{1,0:T(1,128)} %attn_gain_ref.1) | copy-start | bytes 24580
  5.8 0.7 %copy-start.5 = (s32[1,64,2]{1,2,0:T(2,128)S(1)}, s32[1,64,2]{1,2,0:T(2,128)}, u32[]{:S(2)}) copy-start(s32[1,64,2]{1,2,0:T(2,128)} %param.13) | copy-start | bytes 1540
  6.5 0.7 %copy-start.6 = (s32[1,64,2]{1,2,0:T(2,128)S(1)}, s32[1,64,2]{1,2,0:T(2,128)}, u32[]{:S(2)}) copy-start(s32[1,64,2]{1,2,0:T(2,128)} %param.14) | copy-start | bytes 1540
  7.2 0.7 %copy-start.7 = (s32[1,6]{1,0:T(1,128)S(1)}, s32[1,6]{1,0:T(1,128)}, u32[]{:S(2)}) copy-start(s32[1,6]{1,0:T(1,128)} %src_ref.1) | copy-start | bytes 76
  7.8 0.7 %copy-start.8 = (s32[1,6]{1,0:T(1,128)S(1)}, s32[1,6]{1,0:T(1,128)}, u32[]{:S(2)}) copy-start(s32[1,6]{1,0:T(1,128)} %target_ref.1) | copy-start | bytes 76
  8.5 0.7 %copy-start.9 = (s32[64]{0:T(128)S(1)}, s32[64]{0:T(128)}, u32[]{:S(2)}) copy-start(s32[64]{0:T(128)} %param.23) | copy-start | bytes 772

commit v4 on v3

--- a/solution.py
+++ b/solution.py
@@ -149,9 +149,10 @@
 
 
 def kernel(
-    rows_ref, route_ref, gate_ref, moe_gain_ref, attn_gain_ref, src_ref, target_ref, cache_len_ref,
+    rows_hbm, route_hbm, gate_hbm, moe_gain_hbm, attn_gain_hbm, src_hbm, target_hbm, cache_len_hbm,
     w_in_hbm, w_out_hbm, attn_hbm, cache_hbm,
     moe_ref, step_ref,
+    rows_ref, route_ref, gate_ref, moe_gain_ref, attn_gain_ref, src_ref, target_ref, cache_len_ref,
     attn_pairs, cache_pairs, attn, cache, w_in, w_out, gathered, hidden, part, part_got, summed, back_got, moe, meta,
     kv, kv_got, mixed, mixed_got, final,
     load_sem, z_send, z_recv, m_send, m_recv, f_send, f_recv, p_send, p_recv, b_send, b_recv,
@@ -177,7 +178,17 @@
         pltpu.make_async_copy(attn_hbm, attn_pairs, load_sem.at[2]),
         pltpu.make_async_copy(cache_hbm, cache_pairs, load_sem.at[3]),
     ]
+    small = (
+        (rows_hbm, rows_ref), (moe_gain_hbm, moe_gain_ref), (src_hbm, src_ref),
+        (target_hbm, target_ref), (route_hbm, route_ref), (gate_hbm, gate_ref),
+        (attn_gain_hbm, attn_gain_ref), (cache_len_hbm, cache_len_ref),
+    )
+    small_loads = [
+        pltpu.make_async_copy(far, near, load_sem.at[4 + i]) for i, (far, near) in enumerate(small)
+    ]
     barrier = pltpu.get_barrier_semaphore()
+    for load in small_loads:
+        load.start()
     friends = [(g, ahead[d], m) for d in range(1, n_expert)]
     friends += [(g, e, mp_peer[j]) for j in (1, 2, 3)]
     friends += [(1 - g, ahead[d], m) for d in range(n_expert)]
@@ -216,6 +227,8 @@
         copy.start()
         pending.append(copy)
 
+    for load in small_loads:
+        load.wait()
     base = rows_ref[0].astype(jnp.float32)
     gathered[block(0), :] = norm_rows(base, moe_gain_ref[...])
     meta[0] = jnp.zeros(meta.shape[1:], jnp.int32)
@@ -466,14 +479,19 @@
     bf16 = jnp.bfloat16
     dma = pltpu.SemaphoreType.DMA
     vmem = pl.BlockSpec(memory_space=pltpu.VMEM)
-    hbm = pl.BlockSpec(memory_space=pl.ANY)
+    hbm = pl.BlockSpec(memory_space=pltpu.HBM)
+    near = [
+        rows, route.transpose(0, 2, 1), gate_int.transpose(0, 2, 1), moe_gain, attn_gain, src_len,
+        target, cache_len.reshape(1, -1),
+    ]
     flops = 4 * total * width * units
     return pl.pallas_call(
         kernel,
         out_shape=(jax.ShapeDtypeStruct(rows.shape, bf16), jax.ShapeDtypeStruct(rows.shape, bf16)),
-        in_specs=[vmem] * 8 + [hbm] * 4,
+        in_specs=[hbm] * 12,
         out_specs=(vmem, vmem),
         scratch_shapes=[
+            *[pltpu.VMEM(array.shape, array.dtype) for array in near],
             pltpu.VMEM(attn.shape, bf16),
             pltpu.VMEM(kv_cache.shape, bf16),
             pltpu.VMEM((width, both), bf16),
@@ -493,7 +511,7 @@
             pltpu.VMEM((4, row_count, quarter), bf16),
             pltpu.VMEM((4, row_count, quarter), bf16),
             pltpu.VMEM((row_count, width), bf16),
-            dma((4,)),
+            dma((12,)),
             dma((n_expert,)), dma((n_expert,)),
             dma((n_expert,)), dma((n_expert,)),
             dma((n_expert, 4)), dma((n_expert, 4)),
@@ -505,12 +523,11 @@
             dma((4,)), dma((4,)),
         ],
         compiler_params=pltpu.CompilerParams(
-            collective_id=0, has_side_effects=True, vmem_limit_bytes=48 * 1024 * 1024
+            collective_id=0, has_side_effects=True, vmem_limit_bytes=63 * 1024 * 1024
         ),
         cost_estimate=pl.CostEstimate(flops=flops, bytes_accessed=12 << 20, transcendentals=0),
     )(
-        rows, route.transpose(0, 2, 1), gate_int.transpose(0, 2, 1), moe_gain, attn_gain, src_len,
-        target, cache_len.reshape(1, -1), w_in, w_out, attn, kv_cache,
+        *near, w_in, w_out, attn, kv_cache,
     )
 
 

time: 64.1 us -> 58 us (0.905)
  local copies, waits for them, and re-layouts: 9.88 us -> 3.34 us
  Pallas kernels: 53.2 us -> 53.9 us
    unnamed x22 -> x2, local copies, waits for them, and re-layouts: 9.88 us -> 3.34 us
    pallas_call x1, Pallas kernels: 53.2 us -> 53.9 us  [dense_body(): pl.pallas_call(kernel, out_shape=(jax.ShapeDtypeStruct(rows.shape, bf16),...]
where the time goes in v4:
time: 58 us; the launch traced here: 57.9 us
  Pallas kernels  53.9 us (93%)
  local copies, waits for them, and re-layouts  3.34 us (6%)
  between operations  0.64 us (1%)
    pallas_call x1, Pallas kernels, dense_body(): pl.pallas_call(kernel, out_shape=(jax.ShapeDtypeStruct(rows.shape, bf16),...  53.9 us
    unnamed x2, local copies, waits for them, and re-layouts  3.34 us

profile of v4, /device:TPU:1, one launch (start us, length us, event | category | flops | bytes accessed | tf_op | source)
XLA Modules:
  0.0 57.9 jit_solution(16273966287668709840)
XLA Ops:
  0.6 53.9 %shard_map.131 = (bf16[1,64,2048]{2,1,0:T(8,128)(2,1)}, bf16[1,64,2048]{2,1,0:T(8,128)(2,1)}) custom-call(bf16[1,64,2048]{2,1,0:T(8,128)(2,1)} %rows_hbm.1, s32[1,2,64]{2,1,0:T(2,128)} %bitcast.7, s32[1,2,64]{2,1,0:T(2,128)} %bitcast.8, f32[1,2048]{1,0:T(1,128)} %moe_gain_hbm.1, f32[1,2048]{1,0:T(1,128)} %attn_gain_hbm.1, s32[1,6]{1,0:T(1,128)} %src_hbm.1, ...), custom_call_target="tpu_custom_call" | custom-call | flops 2147483648 | bytes 12582912 | tf_op jit(solution)/shard_map/pallas_call | solution.py:488
  54.5 1.7 %copy.16 = bf16[1,64,2048]{2,1,0:T(8,128)(2,1)} copy(bf16[1,64,2048]{2,1,0:T(8,128)(2,1)} %get-tuple-element.4) | data formatting | bytes 524288
  56.2 1.7 %copy.17 = bf16[1,64,2048]{2,1,0:T(8,128)(2,1)} copy(bf16[1,64,2048]{2,1,0:T(8,128)(2,1)} %get-tuple-element.5) | data formatting | bytes 524288
